TPU v7x, 32 devices: a whole 2x2x4 slice. The times are simulated.
32 devices in a mesh: row: 8 (over z, y), col: 4 (over x, core).
Axes of the slice: x: 2, y: 2, z: 4, core: 2. Of those that a mesh axis runs over, the one named last changes fastest.
Arguments:
- positions: float32 [16, 3, 32768], P(None, None, 'row'), may hold values from -4 to 4
- vectors: float32 [8, 32768], P(None, 'row'), may hold values from -6 to 6
- pairs: int32 [8, 4, 10, 2], P('row', 'col'), may hold values from 0 to 15, as said below
- valid: int32 [8, 4, 10], P('row', 'col'), may hold values from 0 to 1, as said below
Outputs:
- leading: float32 [8, 32768], P(None, 'row')
Inputs may be any that keep to these rules, and one draw needn't show every extreme that they name: Live slots of a cell come first and name distinct tile pairs with I <= J; no unordered pair of tiles is listed twice in the whole list; padding slots hold 0 0. a < 8, b < 16. `valid`: at most 10 live slots a cell, and some cell has all 10 live.
All inputs are finite; a program needn't handle non-finite values.
Results may differ from a plain program's by a relative error of at most 0.0003.
Values sent between devices are 32-bit elements; how exact they have to be, the bound alone decides.
A program may use at most 128 MiB of HBM per device.

v0:
```python
import functools

import jax
import jax.numpy as jnp
from jax import lax
from jax.experimental import pallas as pl
from jax.experimental.pallas import tpu as pltpu
from jax.sharding import PartitionSpec as P

TILE = 512
GROUP = 8
MESH = pl.DeviceIdType.MESH


def pieces(x):
    high = x.astype(jnp.bfloat16).astype(jnp.float32)
    rest = x - high
    mid = rest.astype(jnp.bfloat16).astype(jnp.float32)
    return high, mid, rest - mid


def stacked(v):
    high = v.astype(jnp.bfloat16).astype(jnp.float32)
    return jnp.concatenate([high, v - high], axis=0).astype(jnp.bfloat16)


def features(x):
    x1, x2, x3 = pieces(x)
    sq = x * x
    norm = -0.5 * (sq[:GROUP] + sq[GROUP : 2 * GROUP] + sq[2 * GROUP :])
    return (x1, x2, x3), jnp.concatenate(pieces(norm), axis=0)


def kernel(
    n_row, n_col, nz, ny, info_ref, x_ref, out_ref, tot_ref,
    far_first, far_last, partial_k, k_high, k_low, to_row, to_col,
    row_sum, col_sum, row_recv, col_recv, own_buf,
    first_row, first_col, second_row, sq_recv, tot_recv,
    ssem, rsem, local_sem,
):
    slots = to_row.shape[0]
    row_tiles = x_ref.shape[0]
    far = (far_first, far_last)
    col_tiles = far_first.shape[0]
    share = col_tiles // n_row
    chunks = len(far)
    depth = 3 * GROUP
    vec_at = chunks * depth
    r = lax.axis_index("row")
    c = lax.axis_index("col")
    z, y = r // ny, r % ny

    barrier = pltpu.get_barrier_semaphore()
    for k in range(1, n_row):
        pl.semaphore_signal(barrier, inc=1, device_id={"row": (r + k) % n_row}, device_id_type=MESH)
    for k in range(1, n_col):
        pl.semaphore_signal(barrier, inc=1, device_id={"col": (c + k) % n_col}, device_id_type=MESH)
    pl.semaphore_wait(barrier, n_row + n_col - 2)

    sends = []
    counter = [0]

    def next_sem():
        counter[0] += 1
        return counter[0] - 1

    def copy(src, dst, at, device):
        return pltpu.make_async_remote_copy(
            src_ref=src, dst_ref=dst, send_sem=ssem.at[at], recv_sem=rsem.at[at],
            device_id=device, device_id_type=MESH,
        )

    def rows_of(chunk):
        if chunk == chunks - 1:
            return pl.ds(chunk * depth, depth + 8)
        return pl.ds(chunk * depth, depth)

    def place(row, chunk):
        return far[chunk].at[pl.ds(row * share, share)]

    def own(chunk):
        return x_ref.at[pl.ds(c * share, share), rows_of(chunk)]

    z_sem = [[next_sem() for _ in range(nz)] for _ in range(chunks)]
    y_sem = [[[next_sem() for _ in range(ny)] for _ in range(nz)] for _ in range(chunks)]

    def z_copy(chunk, k):
        return copy(own(chunk), place(r, chunk), z_sem[chunk][k], {"row": (z + k) % nz * ny + y})

    def z_arrival(chunk, k):
        row = (z - k + nz) % nz * ny + y
        return copy(own(chunk), place(row, chunk), z_sem[chunk][k], {"row": (z + k) % nz * ny + y})

    def y_copy(chunk, k, j):
        row = (z - k + nz) % nz * ny + y
        src = own(chunk) if k == 0 else place(row, chunk)
        return copy(src, place(row, chunk), y_sem[chunk][k][j], {"row": z * ny + (y + j) % ny})

    def y_arrival(chunk, k, j):
        row = (z - k + nz) % nz * ny + (y - j + ny) % ny
        return copy(own(chunk), place(row, chunk), y_sem[chunk][k][j], {"row": z * ny + (y + j) % ny})

    def start_z(chunk):
        for k in reversed(range(1, nz)):
            z_copy(chunk, k).start()
        for j in range(1, ny):
            y_copy(chunk, 0, j).start()

    def forward(chunk, k):
        z_arrival(chunk, k).wait_recv()
        for j in range(1, ny):
            y_copy(chunk, k, j).start()

    def await_y(chunk):
        for k in range(nz):
            for j in range(1, ny):
                y_arrival(chunk, k, j).wait_recv()

    start_z(0)
    for chunk in range(chunks):
        mine = pltpu.make_async_copy(own(chunk), place(r, chunk), local_sem.at[chunk])
        mine.start()
        mine.wait()
    for k in range(1, nz):
        forward(0, k)
    start_z(1)
    await_y(0)

    def apply_slot(slot, near_row, near_col):
        high, low = k_high[slot], k_low[slot]
        vr, vc = stacked(near_row), stacked(near_col)
        nt = (((1,), (1,)), ((), ()))
        nn = (((1,), (0,)), ((), ()))
        dot = functools.partial(lax.dot_general, preferred_element_type=jnp.float32)
        rows = dot(vc, high, nt) + dot(vc, low, nt)
        cols = dot(vr, high, nn) + dot(vr, low, nn)
        to_row[slot] = rows[:8] + rows[8:]
        to_col[slot] = cols[:8] + cols[8:]

    def form(slot, chunk):
        a, b = info_ref[2 * slot], info_ref[2 * slot + 1]
        (x1, x2, x3), nx = features(x_ref[a, chunk * depth : (chunk + 1) * depth])
        (y1, y2, y3), ny_ = features(far[chunk][b, :depth])
        one = jnp.ones((depth, TILE), jnp.float32)
        left = jnp.concatenate([x1, x1, x2, x1, x2, x3, nx, one], axis=0)
        left = jnp.transpose(left).astype(jnp.bfloat16)
        right = jnp.concatenate([y1, y2, y1, y3, y2, y1, one, ny_], axis=0).astype(jnp.bfloat16)
        right = right.reshape(8 * depth // 16, 16, TILE)
        spot = lax.broadcasted_iota(jnp.int32, (16, TILE), 0) % GROUP
        total = None
        for s in range(GROUP):
            keep = jnp.where(spot == s, 1.0, 0.0).astype(jnp.bfloat16)
            part = (right * keep[None]).reshape(8 * depth, TILE)
            term = jnp.exp(jnp.dot(left, part, preferred_element_type=jnp.float32))
            total = term if total is None else total + term
        return total, a, b

    for chunk in range(chunks):
        last = chunk == chunks - 1

        def body(slot, carry, chunk=chunk, last=last):
            total, a, b = form(slot, chunk)
            if chunk > 0:
                total = total + partial_k[slot]
            if not last:
                partial_k[slot] = total
                for k in range(1, nz):
                    at = min(slots - 1, k * slots // nz)

                    @pl.when(slot == at)
                    def _():
                        forward(chunk + 1, k)
            else:
                high = total.astype(jnp.bfloat16)
                k_high[slot] = high
                k_low[slot] = (total - high.astype(jnp.float32)).astype(jnp.bfloat16)
                apply_slot(
                    slot, x_ref[a, vec_at : vec_at + 8], far[chunk][b, depth:]
                )
            return carry

        lax.fori_loop(0, slots, body, 0)
        if not last:
            await_y(chunk + 1)

    def exchange(p):
        arrivals = []
        for t in range(col_tiles):
            acc = jnp.zeros((8, TILE), jnp.float32)
            for slot in range(slots):
                a, b = info_ref[2 * slot], info_ref[2 * slot + 1]
                cross = r * row_tiles + a != b // share * row_tiles + c * share + b % share
                live = info_ref[2 * slots + slot]
                weight = jnp.where((b == t) & cross, live, 0).astype(jnp.float32)
                acc = acc + weight * to_col[slot]
            col_sum[p, t] = acc
        for k in range(1, n_row):
            to = (r + k) % n_row
            one = copy(
                col_sum.at[p, pl.ds(to * share, share)], col_recv.at[p, k], next_sem(), {"row": to}
            )
            one.start()
            arrivals.append(one)
        for t in range(row_tiles):
            acc = jnp.zeros((8, TILE), jnp.float32)
            for slot in range(slots):
                live = info_ref[2 * slots + slot]
                weight = jnp.where(info_ref[2 * slot] == t, live, 0).astype(jnp.float32)
                acc = acc + weight * to_row[slot]
            row_sum[p, t] = acc
        for k in range(1, n_col):
            to = (c + k) % n_col
            one = copy(
                row_sum.at[p, pl.ds(to * share, share)], row_recv.at[p, k], next_sem(), {"col": to}
            )
            one.start()
            arrivals.append(one)
        sends.extend(arrivals)
        total = row_sum[p, pl.ds(c * share, share)] + col_sum[p, pl.ds(r * share, share)]
        for one in arrivals:
            one.wait_recv()
        for k in range(1, n_col):
            total = total + row_recv[p, k]
        for k in range(1, n_row):
            total = total + col_recv[p, k]
        own_buf[p] = total
        return total

    def spread(src, dst_of, axis):
        size, me = (n_row, r) if axis == "row" else (n_col, c)
        arrivals = []
        for k in range(1, size):
            at = next_sem()
            one = copy(src, dst_of(me), at, {axis: (me + k) % size})
            one.start()
            sends.append(one)
            arrivals.append(copy(src, dst_of((me - k + size) % size), at, {axis: (me + k) % size}))
        return arrivals

    total = exchange(0)
    arrivals = spread(own_buf.at[0], lambda i: first_col.at[pl.ds(i * share, share)], "row")
    arrivals += spread(own_buf.at[0], lambda i: first_row.at[pl.ds(i * share, share)], "col")
    first_col[pl.ds(r * share, share)] = total
    first_row[pl.ds(c * share, share)] = total
    for one in arrivals:
        one.wait_recv()

    def again(slot, carry):
        apply_slot(slot, first_row[info_ref[2 * slot]], first_col[info_ref[2 * slot + 1]])
        return carry

    lax.fori_loop(0, slots, again, 0)

    total = exchange(1)
    squares = jnp.sum(jnp.sum(total * total, axis=0), axis=1, keepdims=True)
    sq_recv[r] = jnp.broadcast_to(squares, (8, 128))
    square_arrivals = spread(sq_recv.at[r], lambda i: sq_recv.at[i], "row")
    arrivals = spread(own_buf.at[1], lambda i: second_row.at[pl.ds(i * share, share)], "col")
    second_row[pl.ds(c * share, share)] = total
    for one in square_arrivals:
        one.wait_recv()
    tot_recv[c] = jnp.sum(sq_recv[...], axis=0)
    total_arrivals = spread(tot_recv.at[c], lambda i: tot_recv.at[i], "col")
    for one in arrivals:
        one.wait_recv()
    for t in range(row_tiles):
        out_ref[:, t * TILE : (t + 1) * TILE] = second_row[t]
    for one in total_arrivals:
        one.wait_recv()
    tot_ref[...] = jnp.sum(tot_recv[...], axis=0)

    for chunk in range(chunks):
        for k in range(1, nz):
            z_copy(chunk, k).wait_send()
        for k in range(nz):
            for j in range(1, ny):
                y_copy(chunk, k, j).wait_send()
    for one in sends:
        one.wait_send()


def per_device(n_row, n_col, positions, vectors, pairs, valid):
    snaps, _, block = positions.shape
    row_tiles = block // TILE
    share = row_tiles // n_col
    col_tiles = share * n_row
    slots = pairs.shape[2]
    vec = vectors.shape[0]
    ny = 1
    while ny * ny * 4 <= n_row:
        ny *= 2
    nz = n_row // ny
    chunks = snaps // GROUP
    spread = positions.reshape(chunks, GROUP, 3, block).transpose(0, 2, 1, 3)
    both = jnp.concatenate([spread.reshape(3 * snaps, block), vectors], axis=0)
    depth = both.shape[0]
    tiled = both.reshape(depth, row_tiles, TILE).transpose(1, 0, 2)
    info = jnp.concatenate([pairs.reshape(2 * slots), valid.reshape(slots)])
    copies = chunks * (nz + nz * ny) + 3 * (n_row + n_col) + n_row + 2 * n_col
    f32 = jnp.float32
    vm = pltpu.VMEM
    second, total = pl.pallas_call(
        functools.partial(kernel, n_row, n_col, nz, ny),
        out_shape=(
            jax.ShapeDtypeStruct((vec, block), f32),
            jax.ShapeDtypeStruct((vec, 128), f32),
        ),
        in_specs=[
            pl.BlockSpec(memory_space=pltpu.SMEM),
            pl.BlockSpec(memory_space=pltpu.VMEM),
        ],
        out_specs=[pl.BlockSpec(memory_space=pltpu.VMEM)] * 2,
        scratch_shapes=[
            vm((col_tiles, 3 * GROUP, TILE), f32),
            vm((col_tiles, 3 * GROUP + vec, TILE), f32),
            vm((slots, TILE, TILE), f32),
            vm((slots, TILE, TILE), jnp.bfloat16),
            vm((slots, TILE, TILE), jnp.bfloat16),
            vm((slots, vec, TILE), f32),
            vm((slots, vec, TILE), f32),
            vm((2, row_tiles, vec, TILE), f32),
            vm((2, col_tiles, vec, TILE), f32),
            vm((2, n_col, share, vec, TILE), f32),
            vm((2, n_row, share, vec, TILE), f32),
            vm((2, share, vec, TILE), f32),
            vm((row_tiles, vec, TILE), f32),
            vm((col_tiles, vec, TILE), f32),
            vm((row_tiles, vec, TILE), f32),
            vm((n_row, vec, 128), f32),
            vm((n_col, vec, 128), f32),
            pltpu.SemaphoreType.DMA((copies,)),
            pltpu.SemaphoreType.DMA((copies,)),
            pltpu.SemaphoreType.DMA((chunks,)),
        ],
        compiler_params=pltpu.CompilerParams(
            collective_id=0, has_side_effects=True, vmem_limit_bytes=52 * 2**20
        ),
    )(info, tiled)
    mean = total[:, :1] / (block * n_row)
    return second / jnp.sqrt(mean + 1e-06)


def solution(mesh):
    placed = (
        P(None, None, "row"),
        P(None, "row"),
        P("row", "col", None, None),
        P("row", "col", None),
    )
    body = functools.partial(per_device, mesh.shape["row"], mesh.shape["col"])
    return jax.shard_map(body, mesh=mesh, in_specs=placed, out_specs=P(None, "row"), check_vma=False)
```

profile of v0, /device:TPU:0, one launch (start us, length us, event | category | flops | bytes accessed | tf_op | source)
XLA Modules:
  0.0 97.0 jit_solution(5362447481306847683)
XLA Ops:
  0.0 1.2 %copy.7 = f32[2,8,3,4096]{3,1,2,0:T(8,128)S(1)} copy(f32[2,8,3,4096]{3,1,0,2:T(8,128)} %bitcast.12) | data formatting | bytes 1572864 | tf_op jit(solution)/shard_map/reshape | solution.py:294
  1.2 0.5 copy.9
  1.7 0.0 copy-start
  1.7 0.5 copy.8
  2.1 0.4 copy-done
  2.6 0.0 copy-start.1
  2.6 0.1 maximum_bitcast_fusion.x_ref
  2.6 0.6 copy-done.1
  3.2 0.1 copy.6
  3.3 0.1 reshape.14
  3.4 0.0 copy-start.2
  3.4 0.7 copy-done.2
  4.1 0.1 pad_add_fusion.info_ref
  4.2 92.0 %shard_map.46 = (f32[8,4096]{1,0:T(8,128)S(1)}, f32[8,128]{1,0:T(8,128)S(1)}) custom-call(s32[30]{0:T(128)S(1)} %pad_add_fusion.info_ref, f32[8,56,512]{2,1,0:T(8,128)S(1)} %maximum_bitcast_fusion.x_ref), custom_call_target="tpu_custom_call" | custom-call | tf_op jit(solution)/shard_map/pallas_call | solution.py:302
  96.2 0.1 sqrt_reduce_fusion
  96.3 0.7 broadcast_divide_fusion
Async XLA Ops:
  1.7 0.9 copy-start
  2.6 0.7 copy-start.1
  3.4 0.7 copy-start.2
where the time goes:
time: 97.2 us; the launch traced here: 97 us
  Pallas kernels  92 us (95%)
  local copies, waits for them, and re-layouts  3.97 us (4%)
  other arithmetic  1.02 us (1%)
    pallas_call x1, Pallas kernels, per_device(): pl.pallas_call(functools.partial(kernel, n_row, n_col, nz, ny), out_shape...  92 us
    unnamed x8, local copies, waits for them, and re-layouts  2.24 us

commit v1 on v0

--- a/solution.py
+++ b/solution.py
@@ -28,27 +28,55 @@
     x1, x2, x3 = pieces(x)
     sq = x * x
     norm = -0.5 * (sq[:GROUP] + sq[GROUP : 2 * GROUP] + sq[2 * GROUP :])
-    return (x1, x2, x3), jnp.concatenate(pieces(norm), axis=0)
+    return x1, x2, x3, jnp.concatenate(pieces(norm), axis=0)
+
+
+def halves(rows):
+    parts = [rows[i * GROUP : (i + 1) * GROUP] for i in range(24)]
+    half = GROUP // 2
+    first = lax.broadcasted_iota(jnp.int32, (GROUP, TILE), 0) < half
+    turned = [jnp.concatenate([part[half:], part[:half]], axis=0) for part in parts]
+    fill = jnp.zeros((4 * GROUP, TILE), jnp.float32)
+    early = [jnp.where(first, parts[i], turned[i + 1]) for i in range(0, 24, 2)]
+    late = [jnp.where(first, turned[i], parts[i + 1]) for i in range(0, 24, 2)]
+    return jnp.concatenate(early + [fill], axis=0), jnp.concatenate(late + [fill], axis=0)
 
 
 def kernel(
-    n_row, n_col, nz, ny, info_ref, x_ref, out_ref, tot_ref,
-    far_first, far_last, partial_k, k_high, k_low, to_row, to_col,
+    n_row, n_col, nz, ny, pairs_ref, valid_ref, pos_ref, vec_ref, out_ref, tot_ref,
+    far_early, far_late, far_vec, row_vec, left_ref, partial_k, k_high, k_low, to_row, to_col,
     row_sum, col_sum, row_recv, col_recv, own_buf,
     first_row, first_col, second_row, sq_recv, tot_recv,
-    ssem, rsem, local_sem,
+    weight_ref, ssem, rsem, local_sem,
 ):
     slots = to_row.shape[0]
-    row_tiles = x_ref.shape[0]
-    far = (far_first, far_last)
-    col_tiles = far_first.shape[0]
-    share = col_tiles // n_row
-    chunks = len(far)
+    row_tiles = pos_ref.shape[2] // TILE
+    share = row_tiles // n_col
+    col_tiles = share * n_row
+    far = (far_early, far_late, far_vec)
+    chunks = 2
     depth = 3 * GROUP
-    vec_at = chunks * depth
     r = lax.axis_index("row")
     c = lax.axis_index("col")
     z, y = r // ny, r % ny
+
+    def tile_at(tile):
+        return pl.ds(pl.multiple_of(tile * TILE, TILE), TILE)
+
+    locals_ = []
+    for chunk in range(chunks + 1):
+        for t in range(share):
+            cut = tile_at(c * share + t)
+            src = vec_ref.at[:, cut]
+            if chunk < chunks:
+                src = pos_ref.at[:, pl.ds(chunk * GROUP, GROUP), cut]
+            mine = pltpu.make_async_copy(
+                src, far[chunk].at[r * share + t], local_sem.at[chunk * share + t]
+            )
+            mine.start()
+            locals_.append(mine)
+    for t in range(row_tiles):
+        row_vec[t] = vec_ref[:, t * TILE : (t + 1) * TILE]
 
     barrier = pltpu.get_barrier_semaphore()
     for k in range(1, n_row):
@@ -70,19 +98,14 @@
             device_id=device, device_id_type=MESH,
         )
 
-    def rows_of(chunk):
-        if chunk == chunks - 1:
-            return pl.ds(chunk * depth, depth + 8)
-        return pl.ds(chunk * depth, depth)
-
     def place(row, chunk):
         return far[chunk].at[pl.ds(row * share, share)]
 
     def own(chunk):
-        return x_ref.at[pl.ds(c * share, share), rows_of(chunk)]
-
-    z_sem = [[next_sem() for _ in range(nz)] for _ in range(chunks)]
-    y_sem = [[[next_sem() for _ in range(ny)] for _ in range(nz)] for _ in range(chunks)]
+        return place(r, chunk)
+
+    z_sem = [[next_sem() for _ in range(nz)] for _ in range(chunks + 1)]
+    y_sem = [[[next_sem() for _ in range(ny)] for _ in range(nz)] for _ in range(chunks + 1)]
 
     def z_copy(chunk, k):
         return copy(own(chunk), place(r, chunk), z_sem[chunk][k], {"row": (z + k) % nz * ny + y})
@@ -116,14 +139,38 @@
             for j in range(1, ny):
                 y_arrival(chunk, k, j).wait_recv()
 
+    for mine in locals_:
+        mine.wait()
     start_z(0)
-    for chunk in range(chunks):
-        mine = pltpu.make_async_copy(own(chunk), place(r, chunk), local_sem.at[chunk])
-        mine.start()
-        mine.wait()
-    for k in range(1, nz):
-        forward(0, k)
+    one = jnp.ones((depth, TILE), jnp.float32)
+
+    def prepare(tile, carry):
+        for chunk in range(chunks):
+            x1, x2, x3, nx = features(
+                pos_ref[:, chunk * GROUP : (chunk + 1) * GROUP, tile_at(tile)].reshape(depth, TILE)
+            )
+            rows = jnp.concatenate([x1, x1, x2, x1, x2, x3, nx, one], axis=0)
+            for g, part in enumerate(halves(rows)):
+                left_ref[tile, 2 * chunk + g] = jnp.transpose(part).astype(jnp.bfloat16)
+        for k in range(1, nz):
+
+            @pl.when(tile == k * row_tiles // nz)
+            def _():
+                forward(0, k)
+
+        return carry
+
+    lax.fori_loop(0, row_tiles, prepare, 0)
+    for slot in range(slots):
+        a, b, live = pairs_ref[0, 0, 0, slot], pairs_ref[0, 0, 1, slot], valid_ref[0, 0, slot]
+        cross = r * row_tiles + a != b // share * row_tiles + c * share + b % share
+        both = jnp.where(cross, live, 0)
+        for t in range(row_tiles):
+            weight_ref[t * slots + slot] = jnp.where(a == t, live, 0).astype(jnp.float32)
+        for t in range(col_tiles):
+            weight_ref[(row_tiles + t) * slots + slot] = jnp.where(b == t, both, 0).astype(jnp.float32)
     start_z(1)
+    start_z(2)
     await_y(0)
 
     def apply_slot(slot, near_row, near_col):
@@ -137,62 +184,73 @@
         to_row[slot] = rows[:8] + rows[8:]
         to_col[slot] = cols[:8] + cols[8:]
 
+    def apply_first(slot):
+        a, b = pairs_ref[0, 0, 0, slot], pairs_ref[0, 0, 1, slot]
+        apply_slot(slot, row_vec[a], far_vec[b])
+
     def form(slot, chunk):
-        a, b = info_ref[2 * slot], info_ref[2 * slot + 1]
-        (x1, x2, x3), nx = features(x_ref[a, chunk * depth : (chunk + 1) * depth])
-        (y1, y2, y3), ny_ = features(far[chunk][b, :depth])
-        one = jnp.ones((depth, TILE), jnp.float32)
-        left = jnp.concatenate([x1, x1, x2, x1, x2, x3, nx, one], axis=0)
-        left = jnp.transpose(left).astype(jnp.bfloat16)
-        right = jnp.concatenate([y1, y2, y1, y3, y2, y1, one, ny_], axis=0).astype(jnp.bfloat16)
-        right = right.reshape(8 * depth // 16, 16, TILE)
-        spot = lax.broadcasted_iota(jnp.int32, (16, TILE), 0) % GROUP
-        total = None
-        for s in range(GROUP):
-            keep = jnp.where(spot == s, 1.0, 0.0).astype(jnp.bfloat16)
-            part = (right * keep[None]).reshape(8 * depth, TILE)
-            term = jnp.exp(jnp.dot(left, part, preferred_element_type=jnp.float32))
-            total = term if total is None else total + term
-        return total, a, b
+        a, b = pairs_ref[0, 0, 0, slot], pairs_ref[0, 0, 1, slot]
+        y1, y2, y3, ny_ = features(
+            far[chunk][b].reshape(depth, TILE)
+        )
+        rows = jnp.concatenate([y1, y2, y1, y3, y2, y1, one, ny_], axis=0)
+        spot = lax.broadcasted_iota(jnp.int32, (16, TILE), 0) % 4
+        masked = []
+        for part in halves(rows):
+            part = part.astype(jnp.bfloat16).reshape(8, 16, TILE)
+            for s in range(4):
+                keep = jnp.where(spot == s, 1.0, 0.0).astype(jnp.bfloat16)
+                masked.append((part * keep[None]).reshape(128, TILE))
+        for at in range(0, TILE, 128):
+            cut = slice(at, at + 128)
+            total = None
+            for pair in range(4):
+                two = jnp.concatenate([masked[2 * pair][:, cut], masked[2 * pair + 1][:, cut]], axis=1)
+                left = left_ref[a, 2 * chunk + pair // 2]
+                term = jnp.exp(jnp.dot(left, two, preferred_element_type=jnp.float32))
+                term = term[:, :128] + term[:, 128:]
+                total = term if total is None else total + term
+            if chunk > 0:
+                total = total + partial_k[slot, :, cut]
+            if chunk < chunks - 1:
+                partial_k[slot, :, cut] = total
+            else:
+                high = total.astype(jnp.bfloat16)
+                k_high[slot, :, cut] = high
+                k_low[slot, :, cut] = (total - high.astype(jnp.float32)).astype(jnp.bfloat16)
 
     for chunk in range(chunks):
         last = chunk == chunks - 1
 
         def body(slot, carry, chunk=chunk, last=last):
-            total, a, b = form(slot, chunk)
-            if chunk > 0:
-                total = total + partial_k[slot]
+            if last:
+                apply_first(jnp.maximum(slot - 1, 0))
+            form(slot, chunk)
             if not last:
-                partial_k[slot] = total
                 for k in range(1, nz):
-                    at = min(slots - 1, k * slots // nz)
-
-                    @pl.when(slot == at)
+
+                    @pl.when(slot == min(slots - 1, k * slots // nz))
                     def _():
                         forward(chunk + 1, k)
-            else:
-                high = total.astype(jnp.bfloat16)
-                k_high[slot] = high
-                k_low[slot] = (total - high.astype(jnp.float32)).astype(jnp.bfloat16)
-                apply_slot(
-                    slot, x_ref[a, vec_at : vec_at + 8], far[chunk][b, depth:]
-                )
+                        forward(chunk + 2, k)
+
             return carry
 
-        lax.fori_loop(0, slots, body, 0)
-        if not last:
+        if last:
+            form(0, chunk)
+            lax.fori_loop(1, slots, body, 0)
+            apply_first(slots - 1)
+        else:
+            lax.fori_loop(0, slots, body, 0)
             await_y(chunk + 1)
+            await_y(chunk + 2)
 
     def exchange(p):
         arrivals = []
         for t in range(col_tiles):
             acc = jnp.zeros((8, TILE), jnp.float32)
             for slot in range(slots):
-                a, b = info_ref[2 * slot], info_ref[2 * slot + 1]
-                cross = r * row_tiles + a != b // share * row_tiles + c * share + b % share
-                live = info_ref[2 * slots + slot]
-                weight = jnp.where((b == t) & cross, live, 0).astype(jnp.float32)
-                acc = acc + weight * to_col[slot]
+                acc = acc + weight_ref[(row_tiles + t) * slots + slot] * to_col[slot]
             col_sum[p, t] = acc
         for k in range(1, n_row):
             to = (r + k) % n_row
@@ -204,9 +262,7 @@
         for t in range(row_tiles):
             acc = jnp.zeros((8, TILE), jnp.float32)
             for slot in range(slots):
-                live = info_ref[2 * slots + slot]
-                weight = jnp.where(info_ref[2 * slot] == t, live, 0).astype(jnp.float32)
-                acc = acc + weight * to_row[slot]
+                acc = acc + weight_ref[t * slots + slot] * to_row[slot]
             row_sum[p, t] = acc
         for k in range(1, n_col):
             to = (c + k) % n_col
@@ -246,7 +302,8 @@
         one.wait_recv()
 
     def again(slot, carry):
-        apply_slot(slot, first_row[info_ref[2 * slot]], first_col[info_ref[2 * slot + 1]])
+        a, b = pairs_ref[0, 0, 0, slot], pairs_ref[0, 0, 1, slot]
+        apply_slot(slot, first_row[a], first_col[b])
         return carry
 
     lax.fori_loop(0, slots, again, 0)
@@ -269,7 +326,7 @@
         one.wait_recv()
     tot_ref[...] = jnp.sum(tot_recv[...], axis=0)
 
-    for chunk in range(chunks):
+    for chunk in range(chunks + 1):
         for k in range(1, nz):
             z_copy(chunk, k).wait_send()
         for k in range(nz):
@@ -291,12 +348,7 @@
         ny *= 2
     nz = n_row // ny
     chunks = snaps // GROUP
-    spread = positions.reshape(chunks, GROUP, 3, block).transpose(0, 2, 1, 3)
-    both = jnp.concatenate([spread.reshape(3 * snaps, block), vectors], axis=0)
-    depth = both.shape[0]
-    tiled = both.reshape(depth, row_tiles, TILE).transpose(1, 0, 2)
-    info = jnp.concatenate([pairs.reshape(2 * slots), valid.reshape(slots)])
-    copies = chunks * (nz + nz * ny) + 3 * (n_row + n_col) + n_row + 2 * n_col
+    copies = (chunks + 1) * (nz + nz * ny) + 3 * (n_row + n_col) + n_row + 2 * n_col
     f32 = jnp.float32
     vm = pltpu.VMEM
     second, total = pl.pallas_call(
@@ -307,12 +359,17 @@
         ),
         in_specs=[
             pl.BlockSpec(memory_space=pltpu.SMEM),
+            pl.BlockSpec(memory_space=pltpu.SMEM),
+            pl.BlockSpec(memory_space=pltpu.VMEM),
             pl.BlockSpec(memory_space=pltpu.VMEM),
         ],
         out_specs=[pl.BlockSpec(memory_space=pltpu.VMEM)] * 2,
         scratch_shapes=[
-            vm((col_tiles, 3 * GROUP, TILE), f32),
-            vm((col_tiles, 3 * GROUP + vec, TILE), f32),
+            vm((col_tiles, 3, GROUP, TILE), f32),
+            vm((col_tiles, 3, GROUP, TILE), f32),
+            vm((col_tiles, vec, TILE), f32),
+            vm((row_tiles, vec, TILE), f32),
+            vm((row_tiles, 2 * chunks, TILE, 128), jnp.bfloat16),
             vm((slots, TILE, TILE), f32),
             vm((slots, TILE, TILE), jnp.bfloat16),
             vm((slots, TILE, TILE), jnp.bfloat16),
@@ -328,14 +385,15 @@
             vm((row_tiles, vec, TILE), f32),
             vm((n_row, vec, 128), f32),
             vm((n_col, vec, 128), f32),
+            pltpu.SMEM(((row_tiles + col_tiles) * slots,), f32),
             pltpu.SemaphoreType.DMA((copies,)),
             pltpu.SemaphoreType.DMA((copies,)),
-            pltpu.SemaphoreType.DMA((chunks,)),
+            pltpu.SemaphoreType.DMA(((chunks + 1) * share,)),
         ],
         compiler_params=pltpu.CompilerParams(
             collective_id=0, has_side_effects=True, vmem_limit_bytes=52 * 2**20
         ),
-    )(info, tiled)
+    )(pairs.transpose(0, 1, 3, 2), valid, positions.transpose(1, 0, 2), vectors)
     mean = total[:, :1] / (block * n_row)
     return second / jnp.sqrt(mean + 1e-06)
 

time: 97.2 us -> 92.2 us (0.949)
  Pallas kernels: 92 us -> 88.4 us
  local copies, waits for them, and re-layouts: 3.97 us -> 2.72 us
    pallas_call x1, Pallas kernels: 92 us -> 88.4 us  [per_device(): pl.pallas_call(functools.partial(kernel, n_row, n_col, nz, ny), out_shape...]
    reshape x2 -> x0, local copies, waits for them, and re-layouts: 1.27 us -> none  [the longest x1 1.18 us: per_device(): spread = positions.reshape(chunks, GROUP, 3, block).transpose(0, 2, 1, 3)]
where the time goes in v1:
time: 92.2 us; the launch traced here: 92 us
  Pallas kernels  88.4 us (96%)
  local copies, waits for them, and re-layouts  2.72 us (3%)
    pallas_call x1, Pallas kernels, per_device(): pl.pallas_call(functools.partial(kernel, n_row, n_col, nz, ny), out_shape...  88.4 us
    unnamed x8, local copies, waits for them, and re-layouts  2.72 us

profile of v1, /device:TPU:0, one launch (start us, length us, event | category | flops | bytes accessed | tf_op | source)
XLA Modules:
  0.0 92.0 jit_solution(12573965028748772231)
XLA Ops:
  0.0 0.0 copy-start.2
  0.0 0.0 copy-start.3
  0.0 0.7 copy-done.2
  0.7 0.0 copy-done.3
  0.7 0.0 copy-start
  0.7 1.1 %copy-done = f32[16,3,4096]{2,0,1:T(8,128)S(1)} copy-done((f32[16,3,4096]{2,0,1:T(8,128)S(1)}, f32[16,3,4096]{2,0,1:T(8,128)}, u32[]{:S(2)}) %copy-start) | copy-done | bytes 786456
  1.8 0.0 copy-start.1
  1.8 0.9 copy-done.1
  2.7 88.4 %shard_map.46 = (f32[8,4096]{1,0:T(8,128)S(1)}, f32[8,128]{1,0:T(8,128)S(1)}) custom-call(s32[1,1,2,10]{3,2,1,0:T(2,128)S(1)} %bitcast.3, s32[1,1,10]{2,1,0:T(1,128)S(1)} %copy-done.3, f32[3,16,4096]{2,1,0:T(8,128)S(1)} %bitcast.2, f32[8,4096]{1,0:T(8,128)S(1)} %copy-done.1), custom_call_target="tpu_custom_call" | custom-call | tf_op jit(solution)/shard_map/pallas_call | solution.py:354
  91.1 0.1 sqrt_reduce_fusion
  91.2 0.7 broadcast_divide_fusion
Async XLA Ops:
  0.0 0.7 copy-start.2
  0.0 0.7 copy-start.3
  0.7 1.1 %copy-start = (f32[16,3,4096]{2,0,1:T(8,128)S(1)}, f32[16,3,4096]{2,0,1:T(8,128)}, u32[]{:S(2)}) copy-start(f32[16,3,4096]{2,0,1:T(8,128)} %param.4) | copy-start | bytes 2359300
  1.8 0.9 copy-start.1

commit v2 on v1

--- a/solution.py
+++ b/solution.py
@@ -8,7 +8,8 @@
 from jax.sharding import PartitionSpec as P
 
 TILE = 512
-GROUP = 8
+GROUP = 4
+HALF = TILE // 2
 MESH = pl.DeviceIdType.MESH
 
 
@@ -24,38 +25,48 @@
     return jnp.concatenate([high, v - high], axis=0).astype(jnp.bfloat16)
 
 
-def features(x):
-    x1, x2, x3 = pieces(x)
-    sq = x * x
-    norm = -0.5 * (sq[:GROUP] + sq[GROUP : 2 * GROUP] + sq[2 * GROUP :])
-    return x1, x2, x3, jnp.concatenate(pieces(norm), axis=0)
-
-
-def halves(rows):
-    parts = [rows[i * GROUP : (i + 1) * GROUP] for i in range(24)]
-    half = GROUP // 2
-    first = lax.broadcasted_iota(jnp.int32, (GROUP, TILE), 0) < half
-    turned = [jnp.concatenate([part[half:], part[:half]], axis=0) for part in parts]
-    fill = jnp.zeros((4 * GROUP, TILE), jnp.float32)
-    early = [jnp.where(first, parts[i], turned[i + 1]) for i in range(0, 24, 2)]
-    late = [jnp.where(first, turned[i], parts[i + 1]) for i in range(0, 24, 2)]
-    return jnp.concatenate(early + [fill], axis=0), jnp.concatenate(late + [fill], axis=0)
+def pack(rows):
+    return jnp.concatenate([rows[:, :HALF], rows[:, HALF:]], axis=0)
+
+
+def turn(x):
+    return jnp.concatenate([x[GROUP:], x[:GROUP]], axis=0)
+
+
+def unpack(x):
+    return jnp.concatenate([x, turn(x)], axis=1)
+
+
+def terms(x, left):
+    cut = [pieces(v) for v in x]
+    x1, x2, x3 = ([v[i] for v in cut] for i in range(3))
+    norm = list(pieces(-0.5 * (x[0] * x[0] + x[1] * x[1] + x[2] * x[2])))
+    one = [jnp.ones((2 * GROUP, TILE), jnp.float32)] * 3
+    if left:
+        parts = x1 + x1 + x2 + x1 + x2 + x3 + norm + one
+    else:
+        parts = x1 + x2 + x1 + x3 + x2 + x1 + one + norm
+    first = lax.broadcasted_iota(jnp.int32, (2 * GROUP, TILE), 0) < GROUP
+    fill = jnp.zeros((4 * 2 * GROUP, TILE), jnp.float32)
+    both = [jnp.where(first, parts[i], turn(parts[i + 1])) for i in range(0, 24, 2)]
+    return jnp.concatenate(both + [fill], axis=0)
 
 
 def kernel(
-    n_row, n_col, nz, ny, pairs_ref, valid_ref, pos_ref, vec_ref, out_ref, tot_ref,
-    far_early, far_late, far_vec, row_vec, left_ref, partial_k, k_high, k_low, to_row, to_col,
-    row_sum, col_sum, row_recv, col_recv, own_buf,
-    first_row, first_col, second_row, sq_recv, tot_recv,
-    weight_ref, ssem, rsem, local_sem,
+    n_row, n_col, nz, ny, chunks, pairs_ref, valid_ref, pos_ref, vec_ref, out_ref, tot_ref, *scratch
 ):
+    far_pos = scratch[:chunks]
+    (
+        far_vec, row_vec, left_ref, partial_k, k_high, k_low, to_row, to_col,
+        row_sum, col_sum, row_recv, col_recv, own_buf,
+        first_row, first_col, second_row, sq_recv, tot_recv,
+        weight_ref, ssem, rsem,
+    ) = scratch[chunks:]
     slots = to_row.shape[0]
     row_tiles = pos_ref.shape[2] // TILE
     share = row_tiles // n_col
     col_tiles = share * n_row
-    far = (far_early, far_late, far_vec)
-    chunks = 2
-    depth = 3 * GROUP
+    far = list(far_pos) + [far_vec]
     r = lax.axis_index("row")
     c = lax.axis_index("col")
     z, y = r // ny, r % ny
@@ -63,18 +74,14 @@
     def tile_at(tile):
         return pl.ds(pl.multiple_of(tile * TILE, TILE), TILE)
 
-    locals_ = []
-    for chunk in range(chunks + 1):
-        for t in range(share):
-            cut = tile_at(c * share + t)
-            src = vec_ref.at[:, cut]
-            if chunk < chunks:
-                src = pos_ref.at[:, pl.ds(chunk * GROUP, GROUP), cut]
-            mine = pltpu.make_async_copy(
-                src, far[chunk].at[r * share + t], local_sem.at[chunk * share + t]
-            )
-            mine.start()
-            locals_.append(mine)
+    for t in range(share):
+        cut = tile_at(c * share + t)
+        at = r * share + t
+        for q in range(3):
+            rows = pos_ref[q, :, cut]
+            for chunk in range(chunks):
+                far[chunk][at, q] = pack(rows[chunk * GROUP : (chunk + 1) * GROUP])
+        far_vec[at] = vec_ref[:, cut]
     for t in range(row_tiles):
         row_vec[t] = vec_ref[:, t * TILE : (t + 1) * TILE]
 
@@ -139,19 +146,15 @@
             for j in range(1, ny):
                 y_arrival(chunk, k, j).wait_recv()
 
-    for mine in locals_:
-        mine.wait()
     start_z(0)
-    one = jnp.ones((depth, TILE), jnp.float32)
-
     def prepare(tile, carry):
+        rows = [pos_ref[q, :, tile_at(tile)] for q in range(3)]
         for chunk in range(chunks):
-            x1, x2, x3, nx = features(
-                pos_ref[:, chunk * GROUP : (chunk + 1) * GROUP, tile_at(tile)].reshape(depth, TILE)
-            )
-            rows = jnp.concatenate([x1, x1, x2, x1, x2, x3, nx, one], axis=0)
-            for g, part in enumerate(halves(rows)):
-                left_ref[tile, 2 * chunk + g] = jnp.transpose(part).astype(jnp.bfloat16)
+            at = chunk * GROUP // 8 * 8
+            own_rows = [v[at : at + 8] for v in rows]
+            if chunk * GROUP % 8:
+                own_rows = [turn(v) for v in own_rows]
+            left_ref[tile, chunk] = jnp.transpose(terms(own_rows, True)).astype(jnp.bfloat16)
         for k in range(1, nz):
 
             @pl.when(tile == k * row_tiles // nz)
@@ -170,7 +173,6 @@
         for t in range(col_tiles):
             weight_ref[(row_tiles + t) * slots + slot] = jnp.where(b == t, both, 0).astype(jnp.float32)
     start_z(1)
-    start_z(2)
     await_y(0)
 
     def apply_slot(slot, near_row, near_col):
@@ -190,23 +192,20 @@
 
     def form(slot, chunk):
         a, b = pairs_ref[0, 0, 0, slot], pairs_ref[0, 0, 1, slot]
-        y1, y2, y3, ny_ = features(
-            far[chunk][b].reshape(depth, TILE)
-        )
-        rows = jnp.concatenate([y1, y2, y1, y3, y2, y1, one, ny_], axis=0)
-        spot = lax.broadcasted_iota(jnp.int32, (16, TILE), 0) % 4
+        block = far_pos[chunk][b]
+        right = terms([unpack(block[q]) for q in range(3)], False).astype(jnp.bfloat16)
+        right = right.reshape(8, 16, TILE)
+        spot = lax.broadcasted_iota(jnp.int32, (16, TILE), 0) % GROUP
         masked = []
-        for part in halves(rows):
-            part = part.astype(jnp.bfloat16).reshape(8, 16, TILE)
-            for s in range(4):
-                keep = jnp.where(spot == s, 1.0, 0.0).astype(jnp.bfloat16)
-                masked.append((part * keep[None]).reshape(128, TILE))
+        for s in range(GROUP):
+            keep = jnp.where(spot == s, 1.0, 0.0).astype(jnp.bfloat16)
+            masked.append((right * keep[None]).reshape(128, TILE))
+        left = left_ref[a, chunk]
         for at in range(0, TILE, 128):
             cut = slice(at, at + 128)
             total = None
-            for pair in range(4):
+            for pair in range(2):
                 two = jnp.concatenate([masked[2 * pair][:, cut], masked[2 * pair + 1][:, cut]], axis=1)
-                left = left_ref[a, 2 * chunk + pair // 2]
                 term = jnp.exp(jnp.dot(left, two, preferred_element_type=jnp.float32))
                 term = term[:, :128] + term[:, 128:]
                 total = term if total is None else total + term
@@ -219,31 +218,43 @@
                 k_high[slot, :, cut] = high
                 k_low[slot, :, cut] = (total - high.astype(jnp.float32)).astype(jnp.bfloat16)
 
+    step = 2 if slots % 2 == 0 else 1
+    steps = slots // step
     for chunk in range(chunks):
         last = chunk == chunks - 1
 
-        def body(slot, carry, chunk=chunk, last=last):
+        def body(i, carry, chunk=chunk, last=last):
             if last:
-                apply_first(jnp.maximum(slot - 1, 0))
-            form(slot, chunk)
+                for j in range(step):
+                    apply_first((i - 1) * step + j)
+            for j in range(step):
+                form(i * step + j, chunk)
             if not last:
                 for k in range(1, nz):
 
-                    @pl.when(slot == min(slots - 1, k * slots // nz))
+                    @pl.when(i == min(steps - 1, k * steps // nz))
                     def _():
                         forward(chunk + 1, k)
-                        forward(chunk + 2, k)
+                        if chunk + 2 == chunks:
+                            forward(chunk + 2, k)
+                        if k == nz - 1 and chunk + 2 < chunks:
+                            start_z(chunk + 2)
+                            if chunk + 3 == chunks:
+                                start_z(chunk + 3)
 
             return carry
 
         if last:
-            form(0, chunk)
-            lax.fori_loop(1, slots, body, 0)
-            apply_first(slots - 1)
+            for j in range(step):
+                form(j, chunk)
+            lax.fori_loop(1, steps, body, 0)
+            for j in range(step):
+                apply_first(slots - step + j)
         else:
-            lax.fori_loop(0, slots, body, 0)
+            lax.fori_loop(0, steps, body, 0)
             await_y(chunk + 1)
-            await_y(chunk + 2)
+            if chunk + 2 == chunks:
+                await_y(chunk + 2)
 
     def exchange(p):
         arrivals = []
@@ -301,12 +312,9 @@
     for one in arrivals:
         one.wait_recv()
 
-    def again(slot, carry):
+    for slot in range(slots):
         a, b = pairs_ref[0, 0, 0, slot], pairs_ref[0, 0, 1, slot]
         apply_slot(slot, first_row[a], first_col[b])
-        return carry
-
-    lax.fori_loop(0, slots, again, 0)
 
     total = exchange(1)
     squares = jnp.sum(jnp.sum(total * total, axis=0), axis=1, keepdims=True)
@@ -352,7 +360,7 @@
     f32 = jnp.float32
     vm = pltpu.VMEM
     second, total = pl.pallas_call(
-        functools.partial(kernel, n_row, n_col, nz, ny),
+        functools.partial(kernel, n_row, n_col, nz, ny, chunks),
         out_shape=(
             jax.ShapeDtypeStruct((vec, block), f32),
             jax.ShapeDtypeStruct((vec, 128), f32),
@@ -365,11 +373,10 @@
         ],
         out_specs=[pl.BlockSpec(memory_space=pltpu.VMEM)] * 2,
         scratch_shapes=[
-            vm((col_tiles, 3, GROUP, TILE), f32),
-            vm((col_tiles, 3, GROUP, TILE), f32),
+            *[vm((col_tiles, 3, 2 * GROUP, HALF), f32) for _ in range(chunks)],
             vm((col_tiles, vec, TILE), f32),
             vm((row_tiles, vec, TILE), f32),
-            vm((row_tiles, 2 * chunks, TILE, 128), jnp.bfloat16),
+            vm((row_tiles, chunks, TILE, 128), jnp.bfloat16),
             vm((slots, TILE, TILE), f32),
             vm((slots, TILE, TILE), jnp.bfloat16),
             vm((slots, TILE, TILE), jnp.bfloat16),
@@ -388,7 +395,6 @@
             pltpu.SMEM(((row_tiles + col_tiles) * slots,), f32),
             pltpu.SemaphoreType.DMA((copies,)),
             pltpu.SemaphoreType.DMA((copies,)),
-            pltpu.SemaphoreType.DMA(((chunks + 1) * share,)),
         ],
         compiler_params=pltpu.CompilerParams(
             collective_id=0, has_side_effects=True, vmem_limit_bytes=52 * 2**20

time: 92.2 us -> 88.7 us (0.962)
  Pallas kernels: 88.4 us -> 84.9 us
    pallas_call x1, Pallas kernels: 88.4 us -> 84.9 us  [per_device(): pl.pallas_call(functools.partial(kernel, n_row, n_col, nz, ny, chunks), o...]
where the time goes in v2:
time: 88.7 us; the launch traced here: 88.5 us
  Pallas kernels  84.9 us (96%)
  local copies, waits for them, and re-layouts  2.72 us (3%)
    pallas_call x1, Pallas kernels, per_device(): pl.pallas_call(functools.partial(kernel, n_row, n_col, nz, ny, chunks), o...  84.9 us
    unnamed x8, local copies, waits for them, and re-layouts  2.72 us

profile of v2, /device:TPU:0, one launch (start us, length us, event | category | flops | bytes accessed | tf_op | source)
XLA Modules:
  0.0 88.5 jit_solution(6515836047827150723)
XLA Ops:
  0.0 0.0 copy-start.2
  0.0 0.0 copy-start.3
  0.0 0.7 copy-done.2
  0.7 0.0 copy-done.3
  0.7 0.0 copy-start
  0.7 1.1 %copy-done = f32[16,3,4096]{2,0,1:T(8,128)S(1)} copy-done((f32[16,3,4096]{2,0,1:T(8,128)S(1)}, f32[16,3,4096]{2,0,1:T(8,128)}, u32[]{:S(2)}) %copy-start) | copy-done | bytes 786456
  1.8 0.0 copy-start.1
  1.8 0.9 %copy-done.1 = f32[8,4096]{1,0:T(8,128)S(1)} copy-done((f32[8,4096]{1,0:T(8,128)S(1)}, f32[8,4096]{1,0:T(8,128)}, u32[]{:S(2)}) %copy-start.1) | copy-done | bytes 131096
  2.7 84.9 %shard_map.46 = (f32[8,4096]{1,0:T(8,128)S(1)}, f32[8,128]{1,0:T(8,128)S(1)}) custom-call(s32[1,1,2,10]{3,2,1,0:T(2,128)S(1)} %bitcast.3, s32[1,1,10]{2,1,0:T(1,128)S(1)} %copy-done.3, f32[3,16,4096]{2,1,0:T(8,128)S(1)} %bitcast.2, f32[8,4096]{1,0:T(8,128)S(1)} %copy-done.1), custom_call_target="tpu_custom_call" | custom-call | tf_op jit(solution)/shard_map/pallas_call | solution.py:362
  87.6 0.1 sqrt_reduce_fusion
  87.7 0.7 broadcast_divide_fusion
Async XLA Ops:
  0.0 0.7 copy-start.2
  0.0 0.7 copy-start.3
  0.7 1.1 %copy-start = (f32[16,3,4096]{2,0,1:T(8,128)S(1)}, f32[16,3,4096]{2,0,1:T(8,128)}, u32[]{:S(2)}) copy-start(f32[16,3,4096]{2,0,1:T(8,128)} %param.4) | copy-start | bytes 2359300
  1.8 0.9 %copy-start.1 = (f32[8,4096]{1,0:T(8,128)S(1)}, f32[8,4096]{1,0:T(8,128)}, u32[]{:S(2)}) copy-start(f32[8,4096]{1,0:T(8,128)} %vec_ref.1) | copy-start | bytes 393220

commit v3 on v2

--- a/solution.py
+++ b/solution.py
@@ -10,6 +10,7 @@
 TILE = 512
 GROUP = 4
 HALF = TILE // 2
+ROWS = 64
 MESH = pl.DeviceIdType.MESH
 
 
@@ -190,33 +191,37 @@
         a, b = pairs_ref[0, 0, 0, slot], pairs_ref[0, 0, 1, slot]
         apply_slot(slot, row_vec[a], far_vec[b])
 
+    def put(slot, chunk, rows, cut, total):
+        if chunk > 0:
+            total = total + partial_k[slot, rows, cut]
+        if chunk < chunks - 1:
+            partial_k[slot, rows, cut] = total
+        else:
+            high = total.astype(jnp.bfloat16)
+            k_high[slot, rows, cut] = high
+            k_low[slot, rows, cut] = (total - high.astype(jnp.float32)).astype(jnp.bfloat16)
+
     def form(slot, chunk):
         a, b = pairs_ref[0, 0, 0, slot], pairs_ref[0, 0, 1, slot]
         block = far_pos[chunk][b]
         right = terms([unpack(block[q]) for q in range(3)], False).astype(jnp.bfloat16)
-        right = right.reshape(8, 16, TILE)
-        spot = lax.broadcasted_iota(jnp.int32, (16, TILE), 0) % GROUP
-        masked = []
-        for s in range(GROUP):
-            keep = jnp.where(spot == s, 1.0, 0.0).astype(jnp.bfloat16)
-            masked.append((right * keep[None]).reshape(128, TILE))
         left = left_ref[a, chunk]
-        for at in range(0, TILE, 128):
-            cut = slice(at, at + 128)
-            total = None
-            for pair in range(2):
-                two = jnp.concatenate([masked[2 * pair][:, cut], masked[2 * pair + 1][:, cut]], axis=1)
-                term = jnp.exp(jnp.dot(left, two, preferred_element_type=jnp.float32))
-                term = term[:, :128] + term[:, 128:]
-                total = term if total is None else total + term
-            if chunk > 0:
-                total = total + partial_k[slot, :, cut]
-            if chunk < chunks - 1:
-                partial_k[slot, :, cut] = total
-            else:
-                high = total.astype(jnp.bfloat16)
-                k_high[slot, :, cut] = high
-                k_low[slot, :, cut] = (total - high.astype(jnp.float32)).astype(jnp.bfloat16)
+        spot = lax.broadcasted_iota(jnp.int32, (ROWS, 128), 1) % GROUP
+        keep = [jnp.where(spot == s, 1.0, 0.0).astype(jnp.bfloat16) for s in range(GROUP)]
+        streamed = jnp.concatenate(
+            [left[at : at + ROWS] * mask for at in range(0, TILE, ROWS) for mask in keep], axis=0
+        )
+        for at in range(0, TILE, 256):
+            cut = slice(at, at + 256)
+            exponent = jnp.dot(streamed, right[:, cut], preferred_element_type=jnp.float32)
+            for block_at in range(0, TILE, ROWS):
+                rows = slice(block_at, block_at + ROWS)
+                total = None
+                for s in range(GROUP):
+                    top = block_at * GROUP + s * ROWS
+                    term = jnp.exp(exponent[top : top + ROWS])
+                    total = term if total is None else total + term
+                put(slot, chunk, rows, cut, total)
 
     step = 2 if slots % 2 == 0 else 1
     steps = slots // step

time: 88.7 us -> 90 us (1.015)
  Pallas kernels: 84.9 us -> 86.3 us
    pallas_call x1, Pallas kernels: 84.9 us -> 86.3 us  [per_device(): pl.pallas_call(functools.partial(kernel, n_row, n_col, nz, ny, chunks), o...]
where the time goes in v3:
time: 90 us; the launch traced here: 89.9 us
  Pallas kernels  86.3 us (96%)
  local copies, waits for them, and re-layouts  2.72 us (3%)
    pallas_call x1, Pallas kernels, per_device(): pl.pallas_call(functools.partial(kernel, n_row, n_col, nz, ny, chunks), o...  86.3 us
    unnamed x8, local copies, waits for them, and re-layouts  2.72 us

profile of v3, /device:TPU:0, one launch (start us, length us, event | category | flops | bytes accessed | tf_op | source)
XLA Modules:
  0.0 89.9 jit_solution(3178203005820463313)
XLA Ops:
  0.0 0.0 copy-start.2
  0.0 0.0 copy-start.3
  0.0 0.7 copy-done.2
  0.7 0.0 copy-done.3
  0.7 0.0 copy-start
  0.7 1.1 %copy-done = f32[16,3,4096]{2,0,1:T(8,128)S(1)} copy-done((f32[16,3,4096]{2,0,1:T(8,128)S(1)}, f32[16,3,4096]{2,0,1:T(8,128)}, u32[]{:S(2)}) %copy-start) | copy-done | bytes 786456
  1.8 0.0 copy-start.1
  1.8 0.9 %copy-done.1 = f32[8,4096]{1,0:T(8,128)S(1)} copy-done((f32[8,4096]{1,0:T(8,128)S(1)}, f32[8,4096]{1,0:T(8,128)}, u32[]{:S(2)}) %copy-start.1) | copy-done | bytes 131096
  2.7 86.3 %shard_map.46 = (f32[8,4096]{1,0:T(8,128)S(1)}, f32[8,128]{1,0:T(8,128)S(1)}) custom-call(s32[1,1,2,10]{3,2,1,0:T(2,128)S(1)} %bitcast.3, s32[1,1,10]{2,1,0:T(1,128)S(1)} %copy-done.3, f32[3,16,4096]{2,1,0:T(8,128)S(1)} %bitcast.2, f32[8,4096]{1,0:T(8,128)S(1)} %copy-done.1), custom_call_target="tpu_custom_call" | custom-call | tf_op jit(solution)/shard_map/pallas_call | solution.py:367
  89.0 0.1 sqrt_reduce_fusion
  89.1 0.7 broadcast_divide_fusion
Async XLA Ops:
  0.0 0.7 copy-start.2
  0.0 0.7 copy-start.3
  0.7 1.1 %copy-start = (f32[16,3,4096]{2,0,1:T(8,128)S(1)}, f32[16,3,4096]{2,0,1:T(8,128)}, u32[]{:S(2)}) copy-start(f32[16,3,4096]{2,0,1:T(8,128)} %param.4) | copy-start | bytes 2359300
  1.8 0.9 %copy-start.1 = (f32[8,4096]{1,0:T(8,128)S(1)}, f32[8,4096]{1,0:T(8,128)}, u32[]{:S(2)}) copy-start(f32[8,4096]{1,0:T(8,128)} %vec_ref.1) | copy-start | bytes 393220

commit v4 on v2

--- a/solution.py
+++ b/solution.py
@@ -53,15 +53,16 @@
 
 
 def kernel(
-    n_row, n_col, nz, ny, chunks, pairs_ref, valid_ref, pos_ref, vec_ref, out_ref, tot_ref, *scratch
+    n_row, n_col, nz, ny, chunks, pairs_ref, valid_ref, pos_in, vec_in, out_ref, tot_ref, *scratch
 ):
     far_pos = scratch[:chunks]
+    lefts = scratch[chunks : 2 * chunks]
     (
-        far_vec, row_vec, left_ref, partial_k, k_high, k_low, to_row, to_col,
+        far_vec, row_vec, pos_ref, vec_ref, load_sem, partial_k, k_high, k_low, to_row, to_col,
         row_sum, col_sum, row_recv, col_recv, own_buf,
         first_row, first_col, second_row, sq_recv, tot_recv,
         weight_ref, ssem, rsem,
-    ) = scratch[chunks:]
+    ) = scratch[2 * chunks :]
     slots = to_row.shape[0]
     row_tiles = pos_ref.shape[2] // TILE
     share = row_tiles // n_col
@@ -74,6 +75,20 @@
     def tile_at(tile):
         return pl.ds(pl.multiple_of(tile * TILE, TILE), TILE)
 
+    loads = [
+        pltpu.make_async_copy(pos_in, pos_ref, load_sem.at[0]),
+        pltpu.make_async_copy(vec_in, vec_ref, load_sem.at[1]),
+    ]
+    for load in loads:
+        load.start()
+
+    barrier = pltpu.get_barrier_semaphore()
+    for k in range(1, n_row):
+        pl.semaphore_signal(barrier, inc=1, device_id={"row": (r + k) % n_row}, device_id_type=MESH)
+    for k in range(1, n_col):
+        pl.semaphore_signal(barrier, inc=1, device_id={"col": (c + k) % n_col}, device_id_type=MESH)
+    for load in loads:
+        load.wait()
     for t in range(share):
         cut = tile_at(c * share + t)
         at = r * share + t
@@ -85,11 +100,6 @@
     for t in range(row_tiles):
         row_vec[t] = vec_ref[:, t * TILE : (t + 1) * TILE]
 
-    barrier = pltpu.get_barrier_semaphore()
-    for k in range(1, n_row):
-        pl.semaphore_signal(barrier, inc=1, device_id={"row": (r + k) % n_row}, device_id_type=MESH)
-    for k in range(1, n_col):
-        pl.semaphore_signal(barrier, inc=1, device_id={"col": (c + k) % n_col}, device_id_type=MESH)
     pl.semaphore_wait(barrier, n_row + n_col - 2)
 
     sends = []
@@ -147,23 +157,17 @@
                 y_arrival(chunk, k, j).wait_recv()
 
     start_z(0)
-    def prepare(tile, carry):
-        rows = [pos_ref[q, :, tile_at(tile)] for q in range(3)]
-        for chunk in range(chunks):
-            at = chunk * GROUP // 8 * 8
-            own_rows = [v[at : at + 8] for v in rows]
-            if chunk * GROUP % 8:
-                own_rows = [turn(v) for v in own_rows]
-            left_ref[tile, chunk] = jnp.transpose(terms(own_rows, True)).astype(jnp.bfloat16)
-        for k in range(1, nz):
-
-            @pl.when(tile == k * row_tiles // nz)
-            def _():
-                forward(0, k)
-
-        return carry
-
-    lax.fori_loop(0, row_tiles, prepare, 0)
+    def prepare(tile, chunk):
+        at = chunk * GROUP // 8 * 8
+        own_rows = [pos_ref[q, at : at + 8, tile_at(tile)] for q in range(3)]
+        if chunk * GROUP % 8:
+            own_rows = [turn(v) for v in own_rows]
+        lefts[chunk][tile] = jnp.transpose(terms(own_rows, True)).astype(jnp.bfloat16)
+
+    for tile in range(row_tiles):
+        prepare(tile, 0)
+    for k in range(1, nz):
+        forward(0, k)
     for slot in range(slots):
         a, b, live = pairs_ref[0, 0, 0, slot], pairs_ref[0, 0, 1, slot], valid_ref[0, 0, slot]
         cross = r * row_tiles + a != b // share * row_tiles + c * share + b % share
@@ -200,7 +204,7 @@
         for s in range(GROUP):
             keep = jnp.where(spot == s, 1.0, 0.0).astype(jnp.bfloat16)
             masked.append((right * keep[None]).reshape(128, TILE))
-        left = left_ref[a, chunk]
+        left = lefts[chunk][a]
         for at in range(0, TILE, 128):
             cut = slice(at, at + 128)
             total = None
@@ -230,6 +234,9 @@
             for j in range(step):
                 form(i * step + j, chunk)
             if not last:
+                each = -(-row_tiles // steps)
+                for j in range(each):
+                    prepare(jnp.minimum(i * each + j, row_tiles - 1), chunk + 1)
                 for k in range(1, nz):
 
                     @pl.when(i == min(steps - 1, k * steps // nz))
@@ -368,15 +375,18 @@
         in_specs=[
             pl.BlockSpec(memory_space=pltpu.SMEM),
             pl.BlockSpec(memory_space=pltpu.SMEM),
-            pl.BlockSpec(memory_space=pltpu.VMEM),
-            pl.BlockSpec(memory_space=pltpu.VMEM),
+            pl.BlockSpec(memory_space=pltpu.HBM),
+            pl.BlockSpec(memory_space=pltpu.HBM),
         ],
         out_specs=[pl.BlockSpec(memory_space=pltpu.VMEM)] * 2,
         scratch_shapes=[
             *[vm((col_tiles, 3, 2 * GROUP, HALF), f32) for _ in range(chunks)],
+            *[vm((row_tiles, TILE, 128), jnp.bfloat16) for _ in range(chunks)],
             vm((col_tiles, vec, TILE), f32),
             vm((row_tiles, vec, TILE), f32),
-            vm((row_tiles, chunks, TILE, 128), jnp.bfloat16),
+            vm((3, snaps, block), f32),
+            vm((vec, block), f32),
+            pltpu.SemaphoreType.DMA((2,)),
             vm((slots, TILE, TILE), f32),
             vm((slots, TILE, TILE), jnp.bfloat16),
             vm((slots, TILE, TILE), jnp.bfloat16),

time: 88.7 us -> 89.1 us (level)
  no operation moved by 1% of the time
where the time goes in v4:
time: 89.1 us; the launch traced here: 89 us
  Pallas kernels  85.4 us (96%)
  local copies, waits for them, and re-layouts  2.72 us (3%)
    pallas_call x1, Pallas kernels, per_device(): pl.pallas_call(functools.partial(kernel, n_row, n_col, nz, ny, chunks), o...  85.4 us
    unnamed x8, local copies, waits for them, and re-layouts  2.72 us

profile of v4, /device:TPU:0, one launch (start us, length us, event | category | flops | bytes accessed | tf_op | source)
XLA Modules:
  0.0 89.0 jit_solution(4833694107898018492)
XLA Ops:
  0.0 0.0 copy-start.2
  0.0 0.0 copy-start.3
  0.0 0.7 copy-done.2
  0.7 0.0 copy-done.3
  0.7 0.0 copy-start
  0.7 1.1 %copy-done = f32[16,3,4096]{2,0,1:T(8,128)S(1)} copy-done((f32[16,3,4096]{2,0,1:T(8,128)S(1)}, f32[16,3,4096]{2,0,1:T(8,128)}, u32[]{:S(2)}) %copy-start) | copy-done | bytes 786456
  1.8 0.0 copy-start.1
  1.8 0.9 %copy-done.1 = f32[8,4096]{1,0:T(8,128)S(1)} copy-done((f32[8,4096]{1,0:T(8,128)S(1)}, f32[8,4096]{1,0:T(8,128)}, u32[]{:S(2)}) %copy-start.1) | copy-done | bytes 131096
  2.7 85.4 %shard_map.46 = (f32[8,4096]{1,0:T(8,128)S(1)}, f32[8,128]{1,0:T(8,128)S(1)}) custom-call(s32[1,1,2,10]{3,2,1,0:T(2,128)S(1)} %bitcast.3, s32[1,1,10]{2,1,0:T(1,128)S(1)} %copy-done.3, f32[3,16,4096]{2,1,0:T(8,128)S(1)} %bitcast.2, f32[8,4096]{1,0:T(8,128)S(1)} %copy-done.1), custom_call_target="tpu_custom_call" | custom-call | tf_op jit(solution)/shard_map/pallas_call | solution.py:369
  88.1 0.1 sqrt_reduce_fusion
  88.2 0.7 broadcast_divide_fusion
Async XLA Ops:
  0.0 0.7 copy-start.2
  0.0 0.7 copy-start.3
  0.7 1.1 %copy-start = (f32[16,3,4096]{2,0,1:T(8,128)S(1)}, f32[16,3,4096]{2,0,1:T(8,128)}, u32[]{:S(2)}) copy-start(f32[16,3,4096]{2,0,1:T(8,128)} %param.4) | copy-start | bytes 2359300
  1.8 0.9 %copy-start.1 = (f32[8,4096]{1,0:T(8,128)S(1)}, f32[8,4096]{1,0:T(8,128)}, u32[]{:S(2)}) copy-start(f32[8,4096]{1,0:T(8,128)} %vec_in.1) | copy-start | bytes 393220
